TPU v7x, 32 devices: a whole 2x2x4 slice. The times are simulated.
32 devices in a mesh: req: 8 (over z, x), tp: 4 (over y, core).
Axes of the slice: x: 2, y: 2, z: 4, core: 2. Of those that a mesh axis runs over, the one named last changes fastest.
Arguments:
- query_heads: bfloat16 [7680, 4096], P('req', 'tp'), parts along dimension 0, may hold values from -140 to 140
- normed_key_heads: bfloat16 [7680, 512], P('req', 'tp'), parts along dimension 0, may hold values from -7 to 7
- value_rows_per_head: bfloat16 [7680, 512], P('req', 'tp'), parts along dimension 0, may hold values from -6 to 6
- residual_in: bfloat16 [7680, 2048], P(('req', 'tp')), parts along dimension 0, may hold values from -6 to 6
- out_weight: bfloat16 [4096, 2048], P('tp'), may hold values from -0.09375 to 0.09375
- norm_gain: float32 [2048], replicated, may hold values from 0.3 to 3
- gate_up: bfloat16 [2, 2, 2048, 768], P(None, None, None, 'tp'), may hold values from -0.125 to 0.125
- down_weight: bfloat16 [2, 768, 2048], P(None, 'tp'), may hold values from -0.21875 to 0.21875
- segment_ids: int32 [7680], P('req'), parts along dimension 0, may hold values from 0 to 5, never falling along the last dimension, each value on 1 to 480 neighbouring positions
- expert_ids: int32 [7680, 8], P('req'), parts along dimension 0, may hold values from 0 to 127, all different within a row; in each aligned block of 960 rows (0 to 959, 960 to 1919, ...) at most 75 rows name the same one
- gate_weights: float32 [7680, 8], P('req'), parts along dimension 0, may hold values from 0.05 to 0.8
Outputs:
- layer_out: bfloat16 [7680, 2048], P(('req', 'tp')), parts along dimension 0
There are 8 independent parts, one for each index of `req`. A program takes and returns all parts, laid end to end along the dimension named above; an argument that names none is the same for every part. Nothing has to cross between parts.
Inputs may be any that keep to these rules, and one draw needn't show every extreme that they name: `segment_ids`: segment ids never fall along the tokens; each prompt has 1 to 480 tokens and one has exactly 480. `expert_ids`: the 8 experts of a token are distinct; no expert is chosen by more than 75 tokens of a request group, a bound that some block reaches.
All inputs are finite; a program needn't handle non-finite values.
Results may differ from a plain program's by a relative error of at most 0.0053.
Values may be sent and summed in bfloat16 or wider, within the bound.
A program may use at most 128 MiB of HBM per device.

v0:
```python
import math

import jax
import jax.numpy as jnp
from jax import lax
from jax.sharding import PartitionSpec as P

QUERY_HEADS = 32
KEY_VALUE_HEADS = 4
HEAD_WIDTH = 128
EXPERTS = 128


def positions_of(segment_ids):
    earlier = (segment_ids[None, :] < segment_ids[:, None]).astype(jnp.int32)
    return jnp.arange(segment_ids.shape[0], dtype=jnp.int32) - jnp.sum(earlier, axis=1)


def rotary_tables(vectors, token_positions):
    half_dim = vectors.shape[-1] // 2
    frequency = 1000000.0 ** (-jnp.arange(half_dim, dtype=jnp.float32) / half_dim)
    angles = token_positions.astype(jnp.float32)[:, None] * frequency[None, :]
    cosine = jnp.cos(angles)[:, None, :]
    sine = jnp.sin(angles)[:, None, :]
    first = vectors[..., :half_dim]
    second = vectors[..., half_dim:]
    return jnp.concatenate(
        [first * cosine - second * sine, second * cosine + first * sine], axis=-1
    )


def rms_norm(hidden, gain):
    widened = hidden.astype(jnp.float32)
    factor = lax.rsqrt(jnp.mean(widened * widened, axis=-1, keepdims=True) + 1e-06)
    return (widened * factor * gain).astype(jnp.bfloat16)


def compact(chosen, limit):
    total = chosen.shape[0]
    iota = jnp.arange(total, dtype=jnp.int32)
    ranked = jnp.where(chosen, iota, iota + total)
    order = jnp.argsort(ranked, stable=True)[:limit]
    return (order, chosen[order])


def attend(query_heads, normed_key_heads, value_rows_per_head, segment_ids):
    item_count = segment_ids.shape[0]
    token_positions = positions_of(segment_ids)
    kv_local = normed_key_heads.shape[1] // HEAD_WIDTH
    query_group_width = QUERY_HEADS // KEY_VALUE_HEADS
    queries = rotary_tables(
        query_heads.reshape(item_count, kv_local * query_group_width, HEAD_WIDTH).astype(
            jnp.float32
        ),
        token_positions,
    ).astype(jnp.bfloat16)
    keys_after_rotary = rotary_tables(
        normed_key_heads.reshape(item_count, kv_local, HEAD_WIDTH).astype(jnp.float32),
        token_positions,
    ).astype(jnp.bfloat16)
    values = value_rows_per_head.reshape(item_count, kv_local, HEAD_WIDTH)
    indices = jnp.arange(item_count)
    allowed = (segment_ids[:, None] == segment_ids[None, :]) & (
        indices[None, :] <= indices[:, None]
    )
    factor = 1.0 / math.sqrt(HEAD_WIDTH)
    key_one = keys_after_rotary[:, 0]
    value_one = values[:, 0]

    def one_head(query_one, key_one=key_one, value_one=value_one):
        scores = jnp.dot(query_one, key_one.T, preferred_element_type=jnp.float32) * factor
        scores = jnp.where(allowed, scores, -1e30)
        peak = jnp.max(scores, axis=1, keepdims=True)
        weights = jnp.exp(scores - peak)
        weights = (weights / jnp.sum(weights, axis=1, keepdims=True)).astype(jnp.bfloat16)
        return jnp.dot(weights, value_one, preferred_element_type=jnp.float32).astype(jnp.bfloat16)

    group_queries = queries.transpose(1, 0, 2)
    blocks = lax.map(one_head, group_queries)
    attended = blocks.transpose(1, 0, 2)
    return attended.reshape(item_count, kv_local * query_group_width * HEAD_WIDTH)


def local(
    query_heads,
    normed_key_heads,
    value_rows_per_head,
    residual_in,
    out_weight,
    norm_gain,
    gate_up,
    down_weight,
    segment_ids,
    expert_ids,
    gate_weights,
):
    attended = attend(query_heads, normed_key_heads, value_rows_per_head, segment_ids)
    tok_rows = residual_in.shape[0]
    width = residual_in.shape[1]
    group_tokens = expert_ids.shape[0]
    capacity = group_tokens * expert_ids.shape[1] * 5 // (EXPERTS * 4)
    window = gate_up.shape[0]
    slots = jnp.arange(window, dtype=jnp.int32)
    route_all = jnp.sum(
        jnp.where(expert_ids[:, :, None] == slots[None, None, :], gate_weights[:, :, None], 0.0),
        axis=1,
    )
    normed_all = None
    rows = attended
    projected = lax.psum_scatter(
        jnp.dot(rows, out_weight, preferred_element_type=jnp.float32),
        "tp",
        scatter_dimension=0,
        tiled=True,
    )
    mixed = (residual_in.astype(jnp.float32) + projected).astype(jnp.bfloat16)
    normed = rms_norm(mixed, norm_gain)
    normed_all = lax.all_gather(normed, "tp", axis=0, tiled=True)
    rows = normed_all
    limit = min(capacity, tok_rows * lax.axis_size("tp"))
    summed = jnp.zeros((tok_rows * lax.axis_size("tp"), width), jnp.float32)
    for expert in range(window):
        taken, valid = compact(jnp.any(expert_ids == expert, axis=1), limit)
        picked = rows[taken]
        gate = jnp.dot(picked, gate_up[expert, 0], preferred_element_type=jnp.float32)
        upward = jnp.dot(picked, gate_up[expert, 1], preferred_element_type=jnp.float32)
        active = (jax.nn.silu(gate) * upward).astype(jnp.bfloat16)
        outputs = jnp.dot(active, down_weight[expert], preferred_element_type=jnp.float32)
        scale = jnp.where(valid, route_all[taken, expert], 0.0)
        summed = summed.at[taken].add(scale[:, None] * outputs)
    experts = lax.psum_scatter(summed, "tp", scatter_dimension=0, tiled=True)
    return (mixed.astype(jnp.float32) + experts).astype(jnp.bfloat16)


def solution(mesh):
    placed = (
        P("req", "tp"),
        P("req", "tp"),
        P("req", "tp"),
        P(("req", "tp"), None),
        P("tp", None),
        P(),
        P(None, None, None, "tp"),
        P(None, "tp", None),
        P("req"),
        P("req", None),
        P("req", None),
    )
    return jax.shard_map(
        local, mesh=mesh, in_specs=placed, out_specs=P(("req", "tp"), None), check_vma=False
    )
```

profile of v0, /device:TPU:0, one launch (start us, length us, event | category | flops | bytes accessed | tf_op | source)
XLA Modules:
  0.0 267.5 jit_solution(13829605986756096867)
XLA Ops:
  6.6 1.4 convert_reduce_fusion
  8.0 1.0 bitcast_convert_fusion
  9.0 1.8 multiply_cosine_fusion.1
  10.7 2.3 fusion.49
  13.5 0.9 copy.25
  14.4 1.5 subtract_convert_fusion
  15.9 1.1 maximum_bitcast_fusion
  18.0 25.1 %while.11 = (s32[]{:T(128)}, bf16[8,960,128]{2,1,0:T(8,128)(2,1)}, bf16[8,960,128]{2,1,0:T(8,128)(2,1)S(1)}, bf16[960,128]{1,0:T(8,128)(2,1)S(1)}, bf16[960,128]...) while((s32[]{:T(128)}, bf16[8,960,128]{2,1,0:T(8,128)(2,1)}, ...), condition=%wide.region_4.5_spmd.clone, body=%wide.region_1.4_spmd.clone.sunk | while | flops 482117760 | bytes 12069725 | solution.py:79
  18.0 1.0 fusion.81
  19.6 1.5 fusion.83
  21.1 1.0 fusion.81
  22.1 0.6 fusion.82
  22.7 1.5 fusion.83
  24.3 1.0 fusion.81
  25.9 1.6 fusion.83
  27.4 1.0 fusion.81
  28.4 0.6 fusion.82
  29.0 1.6 fusion.83
  30.6 1.0 fusion.81
  32.2 1.6 fusion.83
  33.7 1.0 fusion.81
  35.3 1.6 fusion.83
  36.9 1.0 fusion.81
  37.9 0.6 fusion.82
  38.5 1.6 fusion.83
  40.0 1.0 fusion.81
  41.6 1.5 fusion.83
  43.1 10.1 %fusion.17 = f32[960,2048]{1,0:T(8,128)} fusion(bf16[1024,2048]{1,0:T(8,128)(2,1)} %param.17, bf16[8,960,128]{2,1,0:T(8,128)(2,1)} %get-tuple-element.39), kind=kOutput, calls=%fused_computation.37 | convolution fusion | flops 4026531840 | bytes 14024704 | tf_op jit(solution)/shard_map/dot_general | solution.py:111
  53.5 71.6 %reduce-scatter.3.cloned.1.call-done = f32[240,2048]{1,0:T(8,128)} async-done(((f32[960,2048]{1,0:T(8,128)}), f32[240,2048]{1,0:T(8,128)}) %reduce-scatter.3.cloned.1.call-update) | async-done | bytes 1966096 | tf_op jit(solution)/shard_map/reduce_scatter | solution.py:110
  125.1 1.9 fusion.13
  127.0 1.2 fusion.15
  128.4 4.4 %sort.32 = (s32[960]{0:T(1024)}, s32[960]{0:T(1024)S(1)}) sort(s32[960]{0:T(1024)S(1)} %get-tuple-element.103, s32[960]{0:T(1024)S(1)} %iota.47), dimensions={0}, to_apply=%region_12.13 | sort | flops 9600 | bytes 15360 | tf_op jit(solution)/shard_map/jit(argsort)/sort | solution.py:42
  132.8 1.3 gather_fusion.3
  134.1 2.0 gather_fusion.4
  136.2 4.4 %sort.31 = (s32[960]{0:T(1024)}, s32[960]{0:T(1024)S(1)}) sort(s32[960]{0:T(1024)S(1)} %get-tuple-element.104, s32[960]{0:T(1024)S(1)} %iota.45), dimensions={0}, to_apply=%region_7.8 | sort | flops 9600 | bytes 15360 | tf_op jit(solution)/shard_map/jit(argsort)/sort | solution.py:42
  140.5 2.0 gather_fusion.1
  142.6 1.3 gather_fusion
  143.9 17.6 %all-gather.2.cloned.1.call-done = bf16[960,2048]{1,0:T(8,128)(2,1)} async-done(((bf16[240,2048]{1,0:T(8,128)(2,1)}), bf16[960,2048]{1,0:T(8,128)(2,1)}) %all-gather.2.cloned.1.call-update) | async-done | bytes 3932176 | tf_op jit(solution)/shard_map/all_gather | solution.py:118
  161.5 3.7 %gather_fusion.2 = bf16[75,2048]{1,0:T(8,128)(2,1)S(1)} fusion(bf16[960,2048]{1,0:T(8,128)(2,1)} %all-gather.2.cloned.1.call-done, s32[1024]{0:T(1024)S(1)} %pad_clamp_fusion.1), kind=kCustom, calls=%fused_computation.2 | custom fusion | bytes 614700 | tf_op jit(solution)/shard_map/gather | solution.py:124
  165.2 1.5 fusion.30
  166.7 3.7 %gather_fusion.5 = bf16[75,2048]{1,0:T(8,128)(2,1)S(1)} fusion(bf16[960,2048]{1,0:T(8,128)(2,1)} %all-gather.2.cloned.1.call-done, s32[1024]{0:T(1024)S(1)} %pad_clamp_fusion), kind=kCustom, calls=%fused_computation.5 | custom fusion | bytes 614700 | tf_op jit(solution)/shard_map/gather | solution.py:124
  170.4 1.5 fusion.25
  171.9 2.1 convolution_multiply_fusion
  174.1 2.1 convolution_multiply_fusion.1
  176.2 5.0 %scatter_custom_fusion = f32[960,2048]{1,0:T(8,128)} fusion(s32[75]{0:T(128)S(1)} %get-tuple-element.92, f32[75,2048]{1,0:T(8,128)S(1)} %convolution_multiply_fusion.1, f32[]{:T(128)} %constant.16.clone.1), kind=kCustom, calls=%fused_computation.23 | custom fusion | flops 153600 | bytes 7864324 | tf_op jit(solution)/shard_map/scatter-add | solution.py:130
  181.3 7.8 %scatter_fusion = f32[960,2048]{1,0:T(8,128)} fusion(f32[960,2048]{1,0:T(8,128)} %scatter_custom_fusion, s32[75]{0:T(128)S(1)} %get-tuple-element.90, f32[75,2048]{1,0:T(8,128)S(1)} %convolution_multiply_fusion), kind=kCustom, calls=%fused_computation.7 | custom fusion | flops 153600 | bytes 1843500 | tf_op jit(solution)/shard_map/scatter-add | solution.py:130
  189.0 69.1 %reduce-scatter.5.cloned.1.call-done = f32[240,2048]{1,0:T(8,128)} async-done(((f32[960,2048]{1,0:T(8,128)}), f32[240,2048]{1,0:T(8,128)}) %reduce-scatter.5.cloned.1.call-update) | async-done | bytes 1966096 | tf_op jit(solution)/shard_map/reduce_scatter | solution.py:131
  258.2 2.7 %fusion.16 = bf16[240,2048]{1,0:T(8,128)(2,1)} fusion(f32[240,2048]{1,0:T(8,128)} %reduce-scatter.5.cloned.1.call-done, bf16[240,2048]{1,0:T(8,128)(2,1)S(1)} %get-tuple-element.94), kind=kLoop, calls=%fused_computation.36 | loop fusion | flops 1474560 | bytes 3932160 | tf_op jit(solution)/shard_map/convert_element_type | solution.py:132
  (43 shorter events, 4.8 us)
Async XLA Ops:
  6.5 6.5 %copy-start = (bf16[960,1024]{1,0:T(8,128)(2,1)S(1)}, bf16[960,1024]{1,0:T(8,128)(2,1)}, u32[]{:S(2)}) copy-start(bf16[960,1024]{1,0:T(8,128)(2,1)} %param.13) | copy-start | bytes 5898244
  6.5 118.6 %reduce-scatter.3.cloned.1.call-start = ((), (), s32[]{:S(2)}) async-start(), calls=%async_computation.2 | async-start | bytes 9830400 | tf_op jit(solution)/shard_map/reduce_scatter | solution.py:110
  17.0 0.7 copy-start.4
  17.0 1.0 copy-start.6
  53.2 71.9 %copy-start.1 = (bf16[240,2048]{1,0:T(8,128)(2,1)S(1)}, bf16[240,2048]{1,0:T(8,128)(2,1)}, u32[]{:S(2)}) copy-start(bf16[240,2048]{1,0:T(8,128)(2,1)} %param.16) | copy-start | bytes 2949124
  53.2 73.8 %copy-start.5 = (f32[2048]{0:T(1024)S(1)}, f32[2048]{0:T(1024)}, u32[]{:S(2)}) copy-start(f32[2048]{0:T(1024)} %param.18) | copy-start | bytes 24580
  53.3 75.1 %copy-start.2 = (s32[960,8]{0,1:T(8,128)S(1)}, s32[960,8]{0,1:T(8,128)}, u32[]{:S(2)}) copy-start(s32[960,8]{0,1:T(8,128)} %param.22) | copy-start | bytes 92164
  53.3 80.8 %copy-start.3 = (f32[960,8]{0,1:T(8,128)S(1)}, f32[960,8]{0,1:T(8,128)}, u32[]{:S(2)}) copy-start(f32[960,8]{0,1:T(8,128)} %param.23) | copy-start | bytes 92164
  53.3 108.2 %all-gather.2.cloned.1.call-start = ((), (), s32[]{:S(2)}) async-start(), calls=%async_computation.3 | async-start | bytes 4915200 | tf_op jit(solution)/shard_map/all_gather | solution.py:118
  128.3 129.9 %reduce-scatter.5.cloned.1.call-start = ((), (), s32[]{:S(2)}) async-start(), calls=%async_computation.4 | async-start | bytes 9830400 | tf_op jit(solution)/shard_map/reduce_scatter | solution.py:131
Sparse Core Ops, SparseCore 0:
  53.4 71.6 reduce-scatter.2
  128.4 33.0 all-gather.1
  189.2 68.9 reduce-scatter.4
where the time goes:
time: 268 us; the launch traced here: 267 us
  waiting for transfers between devices  158 us (59%)
  other arithmetic  41.9 us (16%)
  matrix products  37.8 us (14%)
  local copies, waits for them, and re-layouts  15.8 us (6%)
  between operations  13.4 us (5%)
    reduce_scatter x1, waiting for transfers between devices, local(): lax.psum_scatter(jnp.dot(rows, out_weight, preferred_element_type=jnp.flo...  71.6 us
    reduce_scatter x1, waiting for transfers between devices, local(): experts = lax.psum_scatter(summed, 'tp', scatter_dimension=0, tiled=True)  69.1 us
    all_gather x1, waiting for transfers between devices, local(): normed_all = lax.all_gather(normed, 'tp', axis=0, tiled=True)  17.6 us
    scatter-add x2, other arithmetic, local(): summed = summed.at[taken].add(scale[:, None] * outputs)  12.8 us
    dot_general x8, matrix products, one_head(): jnp.dot(weights, value_one, preferred_element_type=jnp.float32)  12.4 us
    dot_general x1, matrix products, local(): jnp.dot(rows, out_weight, preferred_element_type=jnp.float32)  10.1 us
    sort x2, other arithmetic, compact(): order = jnp.argsort(ranked, stable=True)[:limit]  8.71 us
    dot_general x8, matrix products, one_head(): jnp.dot(query_one, key_one.T, preferred_element_type=jnp.float32) * factor  7.93 us
  transfers between devices with their start and end apart: 3, of which 3 were waited for; matrix products, arithmetic and copies ran while one was open for 6% of the time, Pallas kernels for 0%

commit v1 on v0

v1 whole, which is shorter than its diff:
```python
import functools
import math

import jax
import jax.numpy as jnp
import ml_dtypes
import numpy as np
from jax import lax
from jax.experimental import pallas as pl
from jax.experimental.pallas import tpu as pltpu
from jax.sharding import PartitionSpec as P

QUERY_HEADS = 32
KEY_VALUE_HEADS = 4
HEAD_WIDTH = 128
EXPERTS = 128
SEG_MOST = 480
F32 = jnp.float32
BF16 = jnp.bfloat16
MASKED = -1e30
PIECES = 4
EXP2_SCALE = math.log2(math.e) / math.sqrt(HEAD_WIDTH)


def rotary_rows():
    half = HEAD_WIDTH // 2
    frequency = np.float32(1000000.0) ** (-np.arange(half, dtype=np.float32) / np.float32(half))
    angles = np.arange(SEG_MOST, dtype=np.float32)[:, None] * frequency[None, :].astype(np.float32)
    cosine, sine = np.cos(angles.astype(np.float64)), np.sin(angles.astype(np.float64))
    rows = np.concatenate([cosine, cosine, -sine, sine], axis=1).astype(np.float32)
    high = rows.astype(ml_dtypes.bfloat16)
    low = (rows - high.astype(np.float32)).astype(ml_dtypes.bfloat16)
    return np.concatenate([high, low], axis=1)


def dot(a, b):
    return jnp.dot(a, b, preferred_element_type=F32)


def dot_nt(a, b):
    return lax.dot_general(a, b, (((1,), (1,)), ((), ())), preferred_element_type=F32)


def layer_kernel(
    slots,
    row_ref, col_ref, table_ref, gain_ref, q_ref, k_ref, v_ref,
    res_hbm, ow_hbm, gu_hbm, dw_hbm,
    out_ref,
    res, ow, gu, dw, load_sem,
    q_rot, k_rot, v_ext, cs, bias_sel, bias, attended,
    sel_f, a1_send, a1_recv, a2_send, a2_recv, mixsel, xs, a_ssem, a_rsem,
    b1_send, b1_recv, b2_send, b2_recv, b3_send, b3_recv, own_f, b_ssem, b_rsem,
    y_f, c1_send, c1_recv, c2_send, c2_recv, ysum, c_ssem, c_rsem,
):
    me = lax.axis_index("tp")
    core = lax.rem(me, 2)
    chip = me // 2
    sib = chip * 2 + (1 - core)
    peer = (1 - chip) * 2 + core
    far = (1 - chip) * 2 + (1 - core)
    tokens, width = q_ref.shape
    heads = width // HEAD_WIDTH
    chunk = out_ref.shape[0]
    model = out_ref.shape[1]
    step = model // PIECES
    half = model // 2
    cap = slots // 2
    window = bias.shape[1]

    loads = [
        pltpu.make_async_copy(src, dst, load_sem.at[i])
        for i, (src, dst) in enumerate([(ow_hbm, ow), (res_hbm, res), (gu_hbm, gu), (dw_hbm, dw)])
    ]
    for load in loads:
        load.start()

    barrier = pltpu.get_barrier_semaphore()
    for other in (sib, peer):
        pl.semaphore_signal(
            barrier, inc=1, device_id={"tp": other}, device_id_type=pl.DeviceIdType.MESH
        )

    def remote(src, dst, ssem, rsem, to):
        return pltpu.make_async_remote_copy(
            src_ref=src, dst_ref=dst, send_sem=ssem, recv_sem=rsem,
            device_id={"tp": to}, device_id_type=pl.DeviceIdType.MESH,
        )

    copy_a1 = remote(a1_send, a1_recv, a_ssem.at[0], a_rsem.at[0], sib)
    copy_a2 = remote(a2_send, a2_recv, a_ssem.at[1], a_rsem.at[1], peer)
    copy_a3 = remote(mixsel.at[core], mixsel.at[core], a_ssem.at[2], a_rsem.at[2], sib)
    copy_b1 = [remote(b1_send.at[p], b1_recv.at[p], b_ssem.at[0, p], b_rsem.at[0, p], sib) for p in range(PIECES)]
    copy_b2 = [remote(b2_send.at[p], b2_recv.at[p], b_ssem.at[1, p], b_rsem.at[1, p], peer) for p in range(PIECES)]
    copy_b3 = [remote(b3_send.at[p], b3_recv.at[p], b_ssem.at[2, p], b_rsem.at[2, p], sib) for p in range(PIECES)]
    copy_c1 = remote(c1_send, c1_recv, c_ssem.at[0], c_rsem.at[0], sib)
    copy_c2 = remote(c2_send, c2_recv, c_ssem.at[1], c_rsem.at[1], peer)
    copy_c3 = remote(ysum.at[core], ysum.at[core], c_ssem.at[2], c_rsem.at[2], sib)

    token_col = lax.broadcasted_iota(jnp.int32, (tokens, 1), 0).astype(F32)
    position = token_col - col_ref[:, 0:1]
    places = lax.broadcasted_iota(jnp.int32, (tokens, SEG_MOST), 1).astype(F32)
    looked = dot((position == places).astype(BF16), table_ref[...])
    cs[...] = looked[:, : 2 * HEAD_WIDTH] + looked[:, 2 * HEAD_WIDTH :]

    def rotate(u):
        u = u.astype(F32)
        turned = pltpu.roll(u, HEAD_WIDTH // 2, 1)
        return (u * cs[:, :HEAD_WIDTH] + turned * cs[:, HEAD_WIDTH:]).astype(BF16)

    k_rot[...] = rotate(k_ref[...])
    v_ext[:, :HEAD_WIDTH] = v_ref[...]
    v_ext[:, HEAD_WIDTH:] = jnp.ones((tokens, HEAD_WIDTH), BF16)

    def rotate_head(h, carry):
        lanes = pl.ds(pl.multiple_of(h * HEAD_WIDTH, HEAD_WIDTH), HEAD_WIDTH)
        q_rot[:, lanes] = rotate(q_ref[:, lanes])
        return carry

    lax.fori_loop(0, heads, rotate_head, 0)

    start_row = row_ref[0:1, :]
    lane_tokens = lax.broadcasted_iota(jnp.int32, (cap, tokens), 1).astype(F32)
    slot_col = lax.broadcasted_iota(jnp.int32, (cap, tokens), 0).astype(F32)
    picks, routes = [], []
    for e in range(2):
        hit = row_ref[1 + e : 2 + e, :] == slot_col
        picks.append(hit.astype(F32).astype(BF16))
        routes.append(jnp.sum(jnp.where(hit, row_ref[3 + e : 4 + e, :], 0.0), axis=1, keepdims=True))
        first = jnp.sum(jnp.where(hit, start_row, 0.0), axis=1, keepdims=True)
        last = jnp.sum(jnp.where(hit, lane_tokens, 0.0), axis=1, keepdims=True)
        keep = (lane_tokens >= first) & (lane_tokens <= last)
        bias_sel[e * cap : (e + 1) * cap, :] = jnp.where(keep, 0.0, MASKED)
    pick = jnp.concatenate(picks, axis=0)
    q_sel = dot(pick, q_rot[...]).astype(BF16)

    def attend(query, keys, values, added):
        scores = dot_nt(query, keys) + added
        peak = jnp.max(scores, axis=1, keepdims=True)
        weights = jnp.exp2((scores - peak) * EXP2_SCALE).astype(BF16)
        mixed = dot(weights, values)
        return (mixed[:, :HEAD_WIDTH] / mixed[:, HEAD_WIDTH:]).astype(BF16)

    pl.semaphore_wait(barrier, 2)

    for h in range(heads):
        lanes = slice(h * HEAD_WIDTH, (h + 1) * HEAD_WIDTH)
        attended[:slots, lanes] = attend(q_sel[:, lanes], k_rot[...], v_ext[...], bias_sel[...])
    loads[0].wait()
    loads[1].wait()
    own_tokens = (lax.broadcasted_iota(jnp.int32, (slots, chunk), 1) + me * chunk).astype(F32)
    ident = jnp.sum(jnp.where(pick > 0, jnp.concatenate([lane_tokens, lane_tokens], axis=0) + 1.0, 0.0), axis=1, keepdims=True) - 1.0
    own_pick = (own_tokens == ident).astype(F32).astype(BF16)
    for p in range(PIECES):
        columns = slice(p * step, (p + 1) * step)
        share = dot(attended[:slots, :], ow[:, columns]) + dot(own_pick, res[:, columns])
        inner = p % (PIECES // 2) * step
        sel_f[p * 2 // PIECES, :, inner : inner + step] = share
    a1_send[...] = sel_f[1 - core].astype(BF16)
    copy_a1.start()

    def forward_a():
        copy_a1.wait_recv()
        a2_send[...] = (sel_f[core] + a1_recv[...].astype(F32)).astype(BF16)
        copy_a2.start()

    def attend_chunk(r, hooks):
        base = pl.multiple_of(r * chunk, 16)
        low = pl.multiple_of(jnp.maximum(r * chunk + chunk - window, 0), 16)
        first = col_ref[pl.ds(base, chunk), 0:1]
        query_at = (lax.broadcasted_iota(jnp.int32, (chunk, window), 0) + base).astype(F32)
        key_at = (lax.broadcasted_iota(jnp.int32, (chunk, window), 1) + low).astype(F32)
        bias[...] = jnp.where((key_at >= first) & (key_at <= query_at), 0.0, MASKED)

        def two_heads(i, carry):
            for s in range(2):
                lanes = pl.ds(pl.multiple_of((2 * i + s) * HEAD_WIDTH, HEAD_WIDTH), HEAD_WIDTH)
                attended[:chunk, lanes] = attend(
                    q_rot[pl.ds(base, chunk), lanes],
                    k_rot[pl.ds(low, window), :],
                    v_ext[pl.ds(low, window), :],
                    bias[...],
                )
            return carry

        quarter = heads // 4
        lax.fori_loop(0, quarter, two_heads, 0)
        hooks[0]()
        lax.fori_loop(quarter, heads // 2, two_heads, 0)
        hooks[1]()

    def project(p):
        return dot(attended[:chunk, :], ow[:, p * step : (p + 1) * step])

    def nothing():
        pass

    attend_chunk(far, (forward_a, nothing))
    for p in range(PIECES):
        b1_send[p] = project(p).astype(BF16)
        copy_b1[p].start()

    attend_chunk(peer, (nothing, nothing))
    for p in range(PIECES):
        share = project(p)
        copy_b1[p].wait_recv()
        b2_send[p] = (share + b1_recv[p].astype(F32)).astype(BF16)
        copy_b2[p].start()

    copy_a2.wait_recv()
    mixsel[core] = (a2_send[...].astype(F32) + a2_recv[...].astype(F32)).astype(BF16)
    copy_a3.start()

    def experts():
        copy_a3.wait_recv()
        left, right = mixsel[0].astype(F32), mixsel[1].astype(F32)
        mean = (jnp.sum(left * left, axis=1, keepdims=True) + jnp.sum(right * right, axis=1, keepdims=True)) / model
        scale = lax.rsqrt(mean + 1e-06)
        xs[:, :half] = (left * scale * gain_ref[:, :half]).astype(BF16)
        xs[:, half:] = (right * scale * gain_ref[:, half:]).astype(BF16)
        loads[2].wait()
        loads[3].wait()
        for e in range(2):
            rows = slice(e * cap, (e + 1) * cap)
            gate = dot(xs[rows, :], gu[e, 0])
            upward = dot(xs[rows, :], gu[e, 1])
            active = (gate / (1.0 + jnp.exp(-gate)) * upward).astype(BF16)
            for s in range(2):
                y_f[s, rows, :] = dot(active, dw[e, :, s * half : (s + 1) * half]) * routes[e]
        c1_send[...] = y_f[1 - core].astype(BF16)
        copy_c1.start()

    def forward_c():
        copy_c1.wait_recv()
        c2_send[...] = (y_f[core] + c1_recv[...].astype(F32)).astype(BF16)
        copy_c2.start()

    attend_chunk(sib, (experts, forward_c))
    for p in range(PIECES):
        b3_send[p] = project(p).astype(BF16)
        copy_b3[p].start()

    attend_chunk(me, (nothing, nothing))
    for p in range(PIECES):
        columns = slice(p * step, (p + 1) * step)
        own_f[p] = project(p) + res[:, columns].astype(F32)

    for p in range(PIECES):
        copy_b3[p].wait_recv()
        copy_b2[p].wait_recv()
        own_f[p] = own_f[p] + b3_recv[p].astype(F32) + b2_recv[p].astype(F32)

    copy_c2.wait_recv()
    ysum[core] = (c2_send[...].astype(F32) + c2_recv[...].astype(F32)).astype(BF16)
    copy_c3.start()

    mine = pl.ds(pl.multiple_of(me * chunk, 16), chunk)
    slot_lane = lax.broadcasted_iota(jnp.int32, (chunk, cap), 1).astype(F32)
    spread = [
        (col_ref[mine, 1 + e : 2 + e] == slot_lane).astype(F32).astype(BF16) for e in range(2)
    ]
    copy_c3.wait_recv()
    for p in range(PIECES):
        inner = p % (PIECES // 2) * step
        side = p * 2 // PIECES
        given = sum(
            dot(spread[e], ysum[side, e * cap : (e + 1) * cap, inner : inner + step])
            for e in range(2)
        )
        mixed = own_f[p].astype(BF16).astype(F32)
        out_ref[:, p * step : (p + 1) * step] = (mixed + given).astype(BF16)

    for copy in [copy_a1, copy_a2, copy_a3, copy_c1, copy_c2, copy_c3] + copy_b1 + copy_b2 + copy_b3:
        copy.wait_send()


def local(
    query_heads,
    normed_key_heads,
    value_rows_per_head,
    residual_in,
    out_weight,
    norm_gain,
    gate_up,
    down_weight,
    segment_ids,
    expert_ids,
    gate_weights,
):
    tokens, width = query_heads.shape
    chunk, model = residual_in.shape
    capacity = tokens * expert_ids.shape[1] * 5 // (EXPERTS * 4)
    cap = -(-capacity // 16) * 16
    slots = 2 * cap
    window = min(tokens, -(-(chunk + SEG_MOST - 1) // 16) * 16)

    index = jnp.arange(tokens, dtype=jnp.int32)
    start = jnp.sum((segment_ids[:, None] < segment_ids[None, :]).astype(F32), axis=0)
    window_ids = jnp.arange(2, dtype=jnp.int32)
    named = expert_ids.T[None, :, :] == window_ids[:, None, None]
    chosen = jnp.any(named, axis=1)
    route = jnp.sum(jnp.where(named, gate_weights.T[None, :, :], 0.0), axis=1)
    before = (index[:, None] < index[None, :]).astype(BF16)
    rank = jnp.dot(chosen.astype(BF16), before, preferred_element_type=F32)
    slot = jnp.where(chosen, rank, -1.0)
    rows = jnp.concatenate([start[None, :], slot, route, jnp.zeros((3, tokens), F32)], axis=0)
    cols = rows.T

    vmem = pl.BlockSpec(memory_space=pltpu.VMEM)
    hbm = pl.BlockSpec(memory_space=pl.ANY)
    step = model // PIECES
    half = model // 2
    dma = pltpu.SemaphoreType.DMA
    pieces = (PIECES, chunk, step)
    scratch = [
        pltpu.VMEM(residual_in.shape, BF16),
        pltpu.VMEM(out_weight.shape, BF16),
        pltpu.VMEM(gate_up.shape, BF16),
        pltpu.VMEM(down_weight.shape, BF16),
        dma((4,)),
        pltpu.VMEM((tokens, width), BF16),
        pltpu.VMEM((tokens, HEAD_WIDTH), BF16),
        pltpu.VMEM((tokens, 2 * HEAD_WIDTH), BF16),
        pltpu.VMEM((tokens, 2 * HEAD_WIDTH), F32),
        pltpu.VMEM((slots, tokens), F32),
        pltpu.VMEM((chunk, window), F32),
        pltpu.VMEM((max(chunk, slots), width), BF16),
        pltpu.VMEM((2, slots, half), F32),
        pltpu.VMEM((slots, half), BF16),
        pltpu.VMEM((slots, half), BF16),
        pltpu.VMEM((slots, half), BF16),
        pltpu.VMEM((slots, half), BF16),
        pltpu.VMEM((2, slots, half), BF16),
        pltpu.VMEM((slots, model), BF16),
        dma((3,)),
        dma((3,)),
        pltpu.VMEM(pieces, BF16),
        pltpu.VMEM(pieces, BF16),
        pltpu.VMEM(pieces, BF16),
        pltpu.VMEM(pieces, BF16),
        pltpu.VMEM(pieces, BF16),
        pltpu.VMEM(pieces, BF16),
        pltpu.VMEM(pieces, F32),
        dma((3, PIECES)),
        dma((3, PIECES)),
        pltpu.VMEM((2, slots, half), F32),
        pltpu.VMEM((slots, half), BF16),
        pltpu.VMEM((slots, half), BF16),
        pltpu.VMEM((slots, half), BF16),
        pltpu.VMEM((slots, half), BF16),
        pltpu.VMEM((2, slots, half), BF16),
        dma((3,)),
        dma((3,)),
    ]
    return pl.pallas_call(
        functools.partial(layer_kernel, slots),
        out_shape=jax.ShapeDtypeStruct((chunk, model), BF16),
        in_specs=[vmem] * 7 + [hbm] * 4,
        out_specs=vmem,
        scratch_shapes=scratch,
        compiler_params=pltpu.CompilerParams(
            collective_id=0, has_side_effects=True, vmem_limit_bytes=56 * 1024 * 1024
        ),
        cost_estimate=pl.CostEstimate(
            flops=14_000_000_000, bytes_accessed=14_000_000, transcendentals=7_000_000
        ),
    )(
        rows, cols, jnp.asarray(rotary_rows()), norm_gain[None, :],
        query_heads, normed_key_heads, value_rows_per_head,
        residual_in, out_weight, gate_up, down_weight,
    )


def solution(mesh):
    placed = (
        P("req", "tp"),
        P("req", "tp"),
        P("req", "tp"),
        P(("req", "tp"), None),
        P("tp", None),
        P(),
        P(None, None, None, "tp"),
        P(None, "tp", None),
        P("req"),
        P("req", None),
        P("req", None),
    )
    return jax.shard_map(
        local, mesh=mesh, in_specs=placed, out_specs=P(("req", "tp"), None), check_vma=False
    )
```

time: 268 us -> 67.8 us (0.25)
  waiting for transfers between devices: 158 us -> 0 us
  Pallas kernels: 0 us -> 54.3 us
  other arithmetic: 41.9 us -> 2.91 us
  matrix products: 37.8 us -> 0.29 us
  between operations: 13.4 us -> 0.02 us
  local copies, waits for them, and re-layouts: 15.8 us -> 9.3 us
    reduce_scatter x2 -> x0, waiting for transfers between devices: 141 us -> none  [the longest x1 71.6 us: local(): lax.psum_scatter(jnp.dot(rows, out_weight, preferred_element_type=jnp.flo...]
    pallas_call x0 -> x1, Pallas kernels: none -> 54.3 us  [local(): pl.pallas_call(functools.partial(layer_kernel, slots), out_shape=jax.Shap...]
    dot_general x21 -> x1, matrix products: 37.8 us -> 0.29 us  [local(): rank = jnp.dot(chosen.astype(BF16), before, preferred_element_type=F32)]
    all_gather x1 -> x0, waiting for transfers between devices: 17.6 us -> none  [local(): normed_all = lax.all_gather(normed, 'tp', axis=0, tiled=True)]
    gather x6 -> x0, local copies, waits for them, and re-layouts: 14 us -> none  [the longest x2 7.37 us: local(): picked = rows[taken]]
    scatter-add x2 -> x0, other arithmetic: 12.8 us -> none  [local(): summed = summed.at[taken].add(scale[:, None] * outputs)]
    sort x2 -> x0, other arithmetic: 8.71 us -> none  [compact(): order = jnp.argsort(ranked, stable=True)[:limit]]
    unnamed x16 -> x4, local copies, waits for them, and re-layouts: 1.76 us -> 8.24 us
  transfers between devices with their start and end apart: 3 -> 0, of which waited for: 3 -> 0; matrix products, arithmetic and copies ran while one was open for 6% -> 0% of each run, Pallas kernels for 0% -> 0%
where the time goes in v1:
time: 67.8 us; the launch traced here: 66.8 us
  Pallas kernels  54.3 us (80%)
  local copies, waits for them, and re-layouts  9.3 us (14%)
  other arithmetic  2.91 us (4%)
    pallas_call x1, Pallas kernels, local(): pl.pallas_call(functools.partial(layer_kernel, slots), out_shape=jax.Shap...  54.3 us
    unnamed x4, local copies, waits for them, and re-layouts  8.24 us

profile of v1, /device:TPU:0, one launch (start us, length us, event | category | flops | bytes accessed | tf_op | source)
XLA Modules:
  0.0 66.8 jit_solution(1303738245309349199)
XLA Ops:
  0.0 0.1 pad.3.clone
  0.1 1.2 %convert_reduce_fusion = f32[960]{0:T(1024)S(1)} fusion(s32[960]{0:T(1024)} %param.20), kind=kLoop, calls=%fused_computation.1 | loop fusion | flops 2763840 | bytes 7680 | tf_op jit(solution)/shard_map/reduce_sum | solution.py:297
  1.3 0.8 %fusion.2 = pred[2,960]{1,0:T(4,128)(4,1)S(1)} fusion(s32[8,960]{1,0:T(8,128)} %bitcast.7), kind=kLoop, calls=%fused_computation.6 | loop fusion | flops 28800 | bytes 32640 | tf_op jit(solution)/shard_map/reduce_or | solution.py:300
  2.1 0.3 fusion.1
  2.4 0.8 %select_reduce_fusion = f32[2,960]{1,0:T(2,128)S(1)} fusion(f32[8,960]{1,0:T(8,128)} %bitcast.9, s32[8,960]{1,0:T(8,128)} %bitcast.8), kind=kLoop, calls=%fused_computation.4 | loop fusion | flops 44160 | bytes 69120 | tf_op jit(solution)/shard_map/reduce_sum | solution.py:301
  3.2 0.1 maximum_maximum_fusion.row_ref
  3.3 0.0 copy-start
  3.3 1.0 %copy.22 = f32[8,960]{0,1:T(8,128)} copy(f32[8,960]{1,0:T(8,128)S(1)} %maximum_maximum_fusion.row_ref) | data formatting | bytes 61440 | tf_op jit(solution)/shard_map/concatenate | solution.py:305
  4.3 6.0 %copy.23.gu_hbm = bf16[2,2,2048,192]{3,2,1,0:T(8,128)(2,1)} copy(bf16[2,2,2048,192]{2,3,1,0:T(8,128)(2,1)} %param.18) | data formatting | bytes 6291456 | tf_op args[6]
  10.3 0.0 copy-done
  10.3 54.3 %shard_map.118 = bf16[240,2048]{1,0:T(8,128)(2,1)} custom-call(f32[8,960]{1,0:T(8,128)} %copy-done, f32[960,8]{1,0:T(8,128)} %bitcast.6, bf16[480,512]{1,0:T(8,128)(2,1)} %constant.3.clone.table_ref, f32[1,2048]{1,0:T(1,128)} %bitcast.11, bf16[960,1024]{1,0:T(8,128)(2,1)} %q_ref.1, bf16[960,128]{1,0:T(8,128)(2,1)} %k_ref.1, bf16[960,128]{1,0:T(8,128)(2,1)} %v_ref.1, ...), custom_call_target="tpu_custom_call" | custom-call | flops 14000000000 | bytes 14000000 | tf_op jit(solution)/shard_map/pallas_call | solution.py:354
  64.6 2.2 %copy.25 = bf16[240,2048]{1,0:T(8,128)(2,1)} copy(bf16[240,2048]{1,0:T(8,128)(2,1)} %shard_map.118) | data formatting | bytes 1966080
  (1 shorter events, 0.0 us)
Async XLA Ops:
  3.3 7.0 %copy-start = (f32[8,960]{1,0:T(8,128)}, f32[8,960]{1,0:T(8,128)S(1)}, u32[]{:S(2)}) copy-start(f32[8,960]{1,0:T(8,128)S(1)} %maximum_maximum_fusion.row_ref) | copy-start | bytes 92164

commit v2 on v1

v2 whole, which is shorter than its diff:
```python
import functools
import math

import jax
import jax.numpy as jnp
import numpy as np
from jax import lax
from jax.experimental import pallas as pl
from jax.experimental.pallas import tpu as pltpu
from jax.sharding import PartitionSpec as P

QUERY_HEADS = 32
KEY_VALUE_HEADS = 4
HEAD_WIDTH = 128
EXPERTS = 128
SEG_MOST = 480
F32 = jnp.float32
BF16 = jnp.bfloat16
MASKED = -1e30
PIECES = 4
HEADS_AT_ONCE = 4
COPIES = 5
EXP2_SCALE = math.log2(math.e) / math.sqrt(HEAD_WIDTH)


def rotary_rows():
    half = HEAD_WIDTH // 2
    frequency = np.float32(1000000.0) ** (-np.arange(half, dtype=np.float32) / np.float32(half))
    angles = np.arange(SEG_MOST, dtype=np.float32)[:, None] * frequency[None, :].astype(np.float32)
    cosine, sine = np.cos(angles.astype(np.float64)), np.sin(angles.astype(np.float64))
    return np.concatenate([cosine, cosine, -sine, sine], axis=1).astype(np.float32)


def dot(a, b):
    return jnp.dot(a, b, preferred_element_type=F32)


def dot_nt(a, b):
    return lax.dot_general(a, b, (((1,), (1,)), ((), ())), preferred_element_type=F32)


def layer_kernel(
    slots, parts,
    seg_ref, ids_ref, gw_ref, table_ref, gain_ref, k_ref, v_ref,
    q_hbm, res_hbm, ow_hbm, gu_hbm, dw_hbm,
    out_ref,
    q, res, ow, gu, dw, load_sem,
    rows_ref, cols_ref, k_rot, v_ext, cs, bias_sel, bias, attended,
    sel_f, a1_send, a1_recv, a2_send, a2_recv, mixsel, xs, a_ssem, a_rsem,
    b1_send, b1_recv, b2_send, b2_recv, b3_send, b3_recv, own_f, b_ssem, b_rsem,
    y_f, c1_send, c1_recv, c2_send, c2_recv, ysum, c_ssem, c_rsem,
):
    me = lax.axis_index("tp")
    core = lax.rem(me, 2)
    chip = me // 2
    sib = chip * 2 + (1 - core)
    peer = (1 - chip) * 2 + core
    far = (1 - chip) * 2 + (1 - core)
    tokens, width = q.shape
    heads = width // HEAD_WIDTH
    chunk, model = out_ref.shape
    step = model // PIECES
    half = model // 2
    cap = slots // 2

    loads = [
        pltpu.make_async_copy(src, dst, load_sem.at[i])
        for i, (src, dst) in enumerate(
            [(q_hbm, q), (ow_hbm, ow), (res_hbm, res), (gu_hbm, gu), (dw_hbm, dw)]
        )
    ]
    for load in loads:
        load.start()

    barrier = pltpu.get_barrier_semaphore()
    for other in (sib, peer):
        pl.semaphore_signal(
            barrier, inc=1, device_id={"tp": other}, device_id_type=pl.DeviceIdType.MESH
        )

    def remote(src, dst, ssem, rsem, to):
        return pltpu.make_async_remote_copy(
            src_ref=src, dst_ref=dst, send_sem=ssem, recv_sem=rsem,
            device_id={"tp": to}, device_id_type=pl.DeviceIdType.MESH,
        )

    def remote_parts(i, src, dst, to):
        return [
            [
                remote(
                    src.at[s, p, pl.ds(0, rows)], dst.at[s, p, pl.ds(0, rows)],
                    b_ssem.at[i, s, p], b_rsem.at[i, s, p], to,
                )
                for p in range(PIECES)
            ]
            for s, (_, rows, _) in enumerate(parts)
        ]

    copy_a1 = remote(a1_send, a1_recv, a_ssem.at[0], a_rsem.at[0], sib)
    copy_a2 = remote(a2_send, a2_recv, a_ssem.at[1], a_rsem.at[1], peer)
    copy_a3 = remote(mixsel.at[core], mixsel.at[core], a_ssem.at[2], a_rsem.at[2], sib)
    copy_b1 = remote_parts(0, b1_send, b1_recv, sib)
    copy_b2 = remote_parts(1, b2_send, b2_recv, peer)
    copy_b3 = remote_parts(2, b3_send, b3_recv, sib)
    copy_c1 = remote(c1_send, c1_recv, c_ssem.at[0], c_rsem.at[0], sib)
    copy_c2 = remote(c2_send, c2_recv, c_ssem.at[1], c_rsem.at[1], peer)
    copy_c3 = remote(ysum.at[core], ysum.at[core], c_ssem.at[2], c_rsem.at[2], sib)

    seg = seg_ref[...]
    prompts = lax.broadcasted_iota(jnp.int32, (8, tokens), 0)
    starts = jnp.sum((seg < prompts).astype(F32), axis=1, keepdims=True)
    start_row = jnp.sum(jnp.where(seg == prompts, starts, 0.0), axis=0, keepdims=True)
    named = [ids_ref[...] == e for e in range(2)]
    chosen = [jnp.max(hit.astype(F32), axis=0, keepdims=True) for hit in named]
    route_rows = [jnp.sum(jnp.where(hit, gw_ref[...], 0.0), axis=0, keepdims=True) for hit in named]
    expert_at = lax.broadcasted_iota(jnp.int32, (16, tokens), 0)
    chosen = jnp.where(expert_at == 0, chosen[0], jnp.where(expert_at == 1, chosen[1], 0.0))
    upper = (
        lax.broadcasted_iota(jnp.int32, (128, 128), 0)
        < lax.broadcasted_iota(jnp.int32, (128, 128), 1)
    ).astype(F32).astype(BF16)
    rows_ref[...] = jnp.zeros_like(rows_ref)
    total = jnp.zeros((16, 1), F32)
    for low in range(0, tokens, 128):
        wide = min(128, tokens - low)
        block = chosen[:, low : low + wide]
        rank = dot(block.astype(BF16), upper[:wide, :wide]) + total
        total = total + jnp.sum(block, axis=1, keepdims=True)
        slot = jnp.where(block > 0, rank, -1.0)[:8]
        line = lax.broadcasted_iota(jnp.int32, (8, wide), 0)
        rows_ref[:, low : low + wide] = jnp.where(line == 2, start_row[:, low : low + wide], slot)
    cols_ref[...] = rows_ref[...].T

    table = table_ref[...]
    high = table.astype(BF16)
    low = (table - high.astype(F32)).astype(BF16)

    def rotary(position):
        places = lax.broadcasted_iota(jnp.int32, (position.shape[0], SEG_MOST), 1).astype(F32)
        at = (position == places).astype(F32).astype(BF16)
        return dot(at, high) + dot(at, low)

    def rotate(u, turn):
        u = u.astype(F32)
        turned = pltpu.roll(u, HEAD_WIDTH // 2, 1)
        return (u * turn[:, :HEAD_WIDTH] + turned * turn[:, HEAD_WIDTH:]).astype(BF16)

    token_col = lax.broadcasted_iota(jnp.int32, (tokens, 1), 0).astype(F32)
    cs[...] = rotary(token_col - cols_ref[:tokens, 2:3])
    k_rot[...] = rotate(k_ref[...], cs[...])
    v_ext[:, :HEAD_WIDTH] = v_ref[...]
    v_ext[:, HEAD_WIDTH:] = jnp.ones((tokens, HEAD_WIDTH), BF16)

    lane_tokens = lax.broadcasted_iota(jnp.int32, (cap, tokens), 1).astype(F32)
    slot_col = lax.broadcasted_iota(jnp.int32, (cap, tokens), 0).astype(F32)
    picks, routes, firsts, lasts, idents = [], [], [], [], []
    for e in range(2):
        hit = rows_ref[e : e + 1, :tokens] == slot_col
        picks.append(hit.astype(F32).astype(BF16))
        routes.append(jnp.sum(jnp.where(hit, route_rows[e], 0.0), axis=1, keepdims=True))
        first = jnp.sum(jnp.where(hit, start_row, 0.0), axis=1, keepdims=True)
        found = jnp.sum(jnp.where(hit, lane_tokens + 1.0, 0.0), axis=1, keepdims=True)
        last = jnp.maximum(found - 1.0, 0.0)
        keep = (lane_tokens >= first) & (lane_tokens <= last)
        bias_sel[e * cap : (e + 1) * cap, :] = jnp.where(keep, 0.0, MASKED)
        firsts.append(first)
        lasts.append(last)
        idents.append(found - 1.0)
    pick = jnp.concatenate(picks, axis=0)
    turn_sel = rotary(jnp.concatenate(lasts, axis=0) - jnp.concatenate(firsts, axis=0))
    loads[0].wait()
    q_sel = dot(pick, q[...])

    def attend(query, keys, values, added):
        scores = dot_nt(query, keys) + added
        peak = jnp.max(scores, axis=1, keepdims=True)
        weights = jnp.exp2((scores - peak) * EXP2_SCALE).astype(BF16)
        mixed = dot(weights, values)
        return (mixed[:, :HEAD_WIDTH] / mixed[:, HEAD_WIDTH:]).astype(BF16)

    for h in range(heads):
        lanes = slice(h * HEAD_WIDTH, (h + 1) * HEAD_WIDTH)
        attended[:slots, lanes] = attend(
            rotate(q_sel[:, lanes], turn_sel), k_rot[...], v_ext[...], bias_sel[...]
        )
    loads[1].wait()
    loads[2].wait()
    own_tokens = (lax.broadcasted_iota(jnp.int32, (slots, chunk), 1) + me * chunk).astype(F32)
    own_pick = (own_tokens == jnp.concatenate(idents, axis=0)).astype(F32).astype(BF16)

    def chosen_share(side):
        columns = pl.ds(pl.multiple_of(side * half, half), half)
        return dot(attended[:slots, :], ow[:, columns]) + dot(own_pick, res[:, columns])

    a1_send[...] = chosen_share(1 - core).astype(BF16)
    pl.semaphore_wait(barrier, 2)
    copy_a1.start()
    sel_f[...] = chosen_share(core)

    def forward_a():
        copy_a1.wait_recv()
        a2_send[...] = (sel_f[...] + a1_recv[...].astype(F32)).astype(BF16)
        copy_a2.start()

    def attend_part(r, s, hooks=()):
        offset, rows, window = parts[s]
        base = pl.multiple_of(r * chunk + offset, 16)
        low = pl.multiple_of(jnp.maximum(r * chunk + (offset + rows - window), 0), 16)
        first = cols_ref[pl.ds(base, rows), 2:3]
        query_at = (lax.broadcasted_iota(jnp.int32, (rows, window), 0) + base).astype(F32)
        key_at = (lax.broadcasted_iota(jnp.int32, (rows, window), 1) + low).astype(F32)
        bias[:rows, :window] = jnp.where((key_at >= first) & (key_at <= query_at), 0.0, MASKED)

        def some_heads(i, carry):
            for n in range(HEADS_AT_ONCE):
                h = i * HEADS_AT_ONCE + n
                lanes = pl.ds(pl.multiple_of(h * HEAD_WIDTH, HEAD_WIDTH), HEAD_WIDTH)
                attended[:rows, lanes] = attend(
                    rotate(q[pl.ds(base, rows), lanes], cs[pl.ds(base, rows), :]),
                    k_rot[pl.ds(low, window), :],
                    v_ext[pl.ds(low, window), :],
                    bias[:rows, :window],
                )
            return carry

        turns = heads // HEADS_AT_ONCE
        if hooks:
            lax.fori_loop(0, turns // 2, some_heads, 0)
            hooks[0]()
            lax.fori_loop(turns // 2, turns, some_heads, 0)
            hooks[1]()
        else:
            lax.fori_loop(0, turns, some_heads, 0)

    def project(s, p):
        return dot(attended[: parts[s][1], :], ow[:, p * step : (p + 1) * step])

    def send_far(s):
        rows = parts[s][1]
        for p in range(PIECES):
            b1_send[s, p, :rows] = project(s, p).astype(BF16)
            copy_b1[s][p].start()

    def send_peer(s):
        rows = parts[s][1]
        for p in range(PIECES):
            share = project(s, p)
            copy_b1[s][p].wait_recv()
            b2_send[s, p, :rows] = (share + b1_recv[s, p, :rows].astype(F32)).astype(BF16)
            copy_b2[s][p].start()

    def nothing():
        pass

    def experts():
        copy_a3.wait_recv()
        left, right = mixsel[0].astype(F32), mixsel[1].astype(F32)
        mean = (
            jnp.sum(left * left, axis=1, keepdims=True)
            + jnp.sum(right * right, axis=1, keepdims=True)
        ) / model
        scale = lax.rsqrt(mean + 1e-06)
        xs[:, :half] = (left * scale * gain_ref[:, :half]).astype(BF16)
        xs[:, half:] = (right * scale * gain_ref[:, half:]).astype(BF16)
        loads[3].wait()
        loads[4].wait()
        for e in range(2):
            rows = slice(e * cap, (e + 1) * cap)
            gate = dot_nt(xs[rows, :], gu[e, 0])
            upward = dot_nt(xs[rows, :], gu[e, 1])
            active = (gate / (1.0 + jnp.exp(-gate)) * upward).astype(BF16)
            for side in range(2):
                y_f[side, rows, :] = dot(active, dw[e, :, side * half : (side + 1) * half]) * routes[e]
        c1_send[...] = y_f[1 - core].astype(BF16)
        copy_c1.start()

    def forward_c():
        copy_c1.wait_recv()
        c2_send[...] = (y_f[core] + c1_recv[...].astype(F32)).astype(BF16)
        copy_c2.start()

    attend_part(far, 0, (forward_a, nothing))
    send_far(0)
    attend_part(peer, 0)
    send_peer(0)
    attend_part(far, 1)
    send_far(1)
    copy_a2.wait_recv()
    mixsel[core] = (a2_send[...].astype(F32) + a2_recv[...].astype(F32)).astype(BF16)
    copy_a3.start()
    attend_part(peer, 1, (experts, forward_c))
    send_peer(1)

    for s in range(len(parts)):
        attend_part(sib, s)
        for p in range(PIECES):
            b3_send[s, p, : parts[s][1]] = project(s, p).astype(BF16)
            copy_b3[s][p].start()
    for s, (offset, rows, _) in enumerate(parts):
        attend_part(me, s)
        for p in range(PIECES):
            columns = slice(p * step, (p + 1) * step)
            own_f[s, p, :rows] = project(s, p) + res[offset : offset + rows, columns].astype(F32)

    copy_c2.wait_recv()
    ysum[core] = (c2_send[...].astype(F32) + c2_recv[...].astype(F32)).astype(BF16)
    copy_c3.start()
    for s, (_, rows, _) in enumerate(parts):
        for p in range(PIECES):
            copy_b3[s][p].wait_recv()
            own_f[s, p, :rows] = own_f[s, p, :rows] + b3_recv[s, p, :rows].astype(F32)
    copy_c3.wait_recv()
    for s, (offset, rows, _) in enumerate(parts):
        mine = pl.ds(pl.multiple_of(me * chunk + offset, 16), rows)
        slot_lane = lax.broadcasted_iota(jnp.int32, (rows, cap), 1).astype(F32)
        spread = [
            (cols_ref[mine, e : e + 1] == slot_lane).astype(F32).astype(BF16) for e in range(2)
        ]
        for p in range(PIECES):
            inner = p % (PIECES // 2) * step
            side = p * 2 // PIECES
            given = sum(
                dot(spread[e], ysum[side, e * cap : (e + 1) * cap, inner : inner + step])
                for e in range(2)
            )
            copy_b2[s][p].wait_recv()
            mixed = own_f[s, p, :rows] + b2_recv[s, p, :rows].astype(F32)
            mixed = mixed.astype(BF16).astype(F32)
            out_ref[offset : offset + rows, p * step : (p + 1) * step] = (mixed + given).astype(BF16)

    for copy in [copy_a1, copy_a2, copy_a3, copy_c1, copy_c2, copy_c3]:
        copy.wait_send()
    for copies in copy_b1 + copy_b2 + copy_b3:
        for copy in copies:
            copy.wait_send()


def hand_over(src, dst, sem):
    rows = src.shape[0] // COPIES
    copies = [
        pltpu.make_async_copy(
            src.at[pl.ds(i * rows, rows)], dst.at[pl.ds(i * rows, rows)], sem.at[i]
        )
        for i in range(COPIES)
    ]
    for copy in copies:
        copy.start()
    for copy in copies:
        copy.wait()


def local(
    query_heads,
    normed_key_heads,
    value_rows_per_head,
    residual_in,
    out_weight,
    norm_gain,
    gate_up,
    down_weight,
    segment_ids,
    expert_ids,
    gate_weights,
):
    tokens, width = query_heads.shape
    chunk, model = residual_in.shape
    capacity = tokens * expert_ids.shape[1] * 5 // (EXPERTS * 4)
    cap = -(-capacity // 16) * 16
    slots = 2 * cap
    first_rows = -(-chunk // 32) * 16
    parts = tuple(
        (offset, rows, min(tokens, -(-(rows + SEG_MOST - 1) // 16) * 16))
        for offset, rows in ((0, first_rows), (first_rows, chunk - first_rows))
    )
    most = max(rows for _, rows, _ in parts)
    window = max(wide for _, _, wide in parts)
    lanes = -(-tokens // 128) * 128


    vmem = pl.BlockSpec(memory_space=pltpu.VMEM)
    hbm = pl.BlockSpec(memory_space=pl.ANY)
    step = model // PIECES
    half = model // 2
    dma = pltpu.SemaphoreType.DMA
    pieces = (2, PIECES, most, step)
    gate_up = jnp.swapaxes(gate_up, 2, 3)
    scratch = [
        pltpu.VMEM((tokens, width), BF16),
        pltpu.VMEM(residual_in.shape, BF16),
        pltpu.VMEM(out_weight.shape, BF16),
        pltpu.VMEM(gate_up.shape, BF16),
        pltpu.VMEM(down_weight.shape, BF16),
        dma((5,)),
        pltpu.VMEM((8, lanes), F32),
        pltpu.VMEM((lanes, 8), F32),
        pltpu.VMEM((tokens, HEAD_WIDTH), BF16),
        pltpu.VMEM((tokens, 2 * HEAD_WIDTH), BF16),
        pltpu.VMEM((tokens, 2 * HEAD_WIDTH), F32),
        pltpu.VMEM((slots, tokens), F32),
        pltpu.VMEM((most, window), F32),
        pltpu.VMEM((max(most, slots), width), BF16),
        pltpu.VMEM((slots, half), F32),
        pltpu.VMEM((slots, half), BF16),
        pltpu.VMEM((slots, half), BF16),
        pltpu.VMEM((slots, half), BF16),
        pltpu.VMEM((slots, half), BF16),
        pltpu.VMEM((2, slots, half), BF16),
        pltpu.VMEM((slots, model), BF16),
        dma((3,)),
        dma((3,)),
        pltpu.VMEM(pieces, BF16),
        pltpu.VMEM(pieces, BF16),
        pltpu.VMEM(pieces, BF16),
        pltpu.VMEM(pieces, BF16),
        pltpu.VMEM(pieces, BF16),
        pltpu.VMEM(pieces, BF16),
        pltpu.VMEM(pieces, F32),
        dma((3, 2, PIECES)),
        dma((3, 2, PIECES)),
        pltpu.VMEM((2, slots, half), F32),
        pltpu.VMEM((slots, half), BF16),
        pltpu.VMEM((slots, half), BF16),
        pltpu.VMEM((slots, half), BF16),
        pltpu.VMEM((slots, half), BF16),
        pltpu.VMEM((2, slots, half), BF16),
        dma((3,)),
        dma((3,)),
    ]
    result = pl.pallas_call(
        functools.partial(layer_kernel, slots, parts),
        out_shape=jax.ShapeDtypeStruct((chunk, model), BF16),
        in_specs=[vmem] * 7 + [hbm] * 5,
        out_specs=vmem,
        scratch_shapes=scratch,
        compiler_params=pltpu.CompilerParams(
            collective_id=0, has_side_effects=True, vmem_limit_bytes=56 * 1024 * 1024
        ),
        cost_estimate=pl.CostEstimate(
            flops=14_000_000_000, bytes_accessed=14_000_000, transcendentals=7_000_000
        ),
    )(
        segment_ids[None, :], expert_ids.T, gate_weights.T, jnp.asarray(rotary_rows()),
        norm_gain[None, :], normed_key_heads, value_rows_per_head,
        query_heads, residual_in, out_weight, gate_up, down_weight,
    )
    return pl.pallas_call(
        hand_over,
        out_shape=jax.ShapeDtypeStruct((chunk, model), BF16),
        in_specs=[hbm],
        out_specs=hbm,
        scratch_shapes=[dma((COPIES,))],
    )(result)


def solution(mesh):
    placed = (
        P("req", "tp"),
        P("req", "tp"),
        P("req", "tp"),
        P(("req", "tp"), None),
        P("tp", None),
        P(),
        P(None, None, None, "tp"),
        P(None, "tp", None),
        P("req"),
        P("req", None),
        P("req", None),
    )
    return jax.shard_map(
        local, mesh=mesh, in_specs=placed, out_specs=P(("req", "tp"), None), check_vma=False
    )
```

time: 67.8 us -> 81 us (1.19); the launches traced: 66.8 us -> 80.9 us
  Pallas kernels: 54.3 us -> 80.7 us
  local copies, waits for them, and re-layouts: 9.3 us -> 0 us
  other arithmetic: 2.91 us -> 0 us
    pallas_call x1 -> x2, Pallas kernels: 54.3 us -> 80.7 us  [the longest x1 49.8 us: local(): pl.pallas_call(functools.partial(layer_kernel, slots, parts), out_shape=j...]
    unnamed x4 -> x0, local copies, waits for them, and re-layouts: 8.24 us -> none
    reduce_sum x2 -> x0, other arithmetic: 2.05 us -> none  [the longest x1 1.23 us: local(): jnp.sum((segment_ids[:, None] < segment_ids[None, :]).astype(F32), axis=0)]
    concatenate x2 -> x0, local copies, waits for them, and re-layouts: 1.06 us -> none  [local(): jnp.concatenate([start[None, :], slot, route, jnp.zeros((3, tokens), F32)...]
where the time goes in v2:
time: 81 us; the launch traced here: 80.9 us
  Pallas kernels  80.7 us (100%)
    pallas_call x1, Pallas kernels, local(): pl.pallas_call(functools.partial(layer_kernel, slots, parts), out_shape=j...  49.8 us
    pallas_call x1, Pallas kernels, local(): pl.pallas_call(hand_over, out_shape=jax.ShapeDtypeStruct((chunk, model),...  30.9 us

profile of v2, /device:TPU:0, one launch (start us, length us, event | category | flops | bytes accessed | tf_op | source)
XLA Modules:
  0.0 80.9 jit_solution(11487626365239039827)
XLA Ops:
  0.0 49.8 %shard_map.118.src = bf16[240,2048]{1,0:T(8,128)(2,1)} custom-call(s32[1,960]{1,0:T(1,128)} %bitcast.9, s32[8,960]{1,0:T(8,128)} %bitcast.6, f32[8,960]{1,0:T(8,128)} %bitcast.7, f32[480,256]{1,0:T(8,128)} %constant.2.clone.table_ref, f32[1,2048]{1,0:T(1,128)} %bitcast.8, bf16[960,128]{1,0:T(8,128)(2,1)} %k_ref.1, bf16[960,128]{1,0:T(8,128)(2,1)} %v_ref.1, ...), custom_call_target="tpu_custom_call" | custom-call | flops 14000000000 | bytes 14000000 | tf_op jit(solution)/shard_map/pallas_call | solution.py:429
  49.8 30.9 %shard_map.119 = bf16[240,2048]{1,0:T(8,128)(2,1)} custom-call(bf16[240,2048]{1,0:T(8,128)(2,1)} %shard_map.118.src), custom_call_target="tpu_custom_call" | custom-call | tf_op jit(solution)/shard_map/pallas_call | solution.py:446

commit v3 on v2

--- a/solution.py
+++ b/solution.py
@@ -101,7 +101,10 @@
     copy_a3 = remote(mixsel.at[core], mixsel.at[core], a_ssem.at[2], a_rsem.at[2], sib)
     copy_b1 = remote_parts(0, b1_send, b1_recv, sib)
     copy_b2 = remote_parts(1, b2_send, b2_recv, peer)
-    copy_b3 = remote_parts(2, b3_send, b3_recv, sib)
+    copy_b3 = [
+        remote(b3_send.at[p], b3_recv.at[p], b_ssem.at[2, 0, p], b_rsem.at[2, 0, p], sib)
+        for p in range(PIECES)
+    ]
     copy_c1 = remote(c1_send, c1_recv, c_ssem.at[0], c_rsem.at[0], sib)
     copy_c2 = remote(c2_send, c2_recv, c_ssem.at[1], c_rsem.at[1], peer)
     copy_c3 = remote(ysum.at[core], ysum.at[core], c_ssem.at[2], c_rsem.at[2], sib)
@@ -171,18 +174,23 @@
     loads[0].wait()
     q_sel = dot(pick, q[...])
 
-    def attend(query, keys, values, added):
-        scores = dot_nt(query, keys) + added
-        peak = jnp.max(scores, axis=1, keepdims=True)
-        weights = jnp.exp2((scores - peak) * EXP2_SCALE).astype(BF16)
-        mixed = dot(weights, values)
-        return (mixed[:, :HEAD_WIDTH] / mixed[:, HEAD_WIDTH:]).astype(BF16)
-
-    for h in range(heads):
-        lanes = slice(h * HEAD_WIDTH, (h + 1) * HEAD_WIDTH)
-        attended[:slots, lanes] = attend(
-            rotate(q_sel[:, lanes], turn_sel), k_rot[...], v_ext[...], bias_sel[...]
-        )
+    def attend(queries, keys, values, added):
+        rows = added.shape[0]
+        scores = dot_nt(jnp.concatenate(queries, axis=0), keys)
+        weights = []
+        for n in range(len(queries)):
+            kept = scores[n * rows : (n + 1) * rows] + added
+            peak = jnp.max(kept, axis=1, keepdims=True)
+            weights.append(jnp.exp2((kept - peak) * EXP2_SCALE).astype(BF16))
+        mixed = dot(jnp.concatenate(weights, axis=0), values)
+        mixed = (mixed[:, :HEAD_WIDTH] / mixed[:, HEAD_WIDTH:]).astype(BF16)
+        return [mixed[n * rows : (n + 1) * rows] for n in range(len(queries))]
+
+    for low in range(0, heads, HEADS_AT_ONCE):
+        lanes = [slice(h * HEAD_WIDTH, (h + 1) * HEAD_WIDTH) for h in range(low, low + HEADS_AT_ONCE)]
+        queries = [rotate(q_sel[:, lane], turn_sel) for lane in lanes]
+        for lane, got in zip(lanes, attend(queries, k_rot[...], v_ext[...], bias_sel[...])):
+            attended[:slots, lane] = got
     loads[1].wait()
     loads[2].wait()
     own_tokens = (lax.broadcasted_iota(jnp.int32, (slots, chunk), 1) + me * chunk).astype(F32)
@@ -202,7 +210,7 @@
         a2_send[...] = (sel_f[...] + a1_recv[...].astype(F32)).astype(BF16)
         copy_a2.start()
 
-    def attend_part(r, s, hooks=()):
+    def attend_part(r, s, hooks=(), at=0):
         offset, rows, window = parts[s]
         base = pl.multiple_of(r * chunk + offset, 16)
         low = pl.multiple_of(jnp.maximum(r * chunk + (offset + rows - window), 0), 16)
@@ -212,15 +220,19 @@
         bias[:rows, :window] = jnp.where((key_at >= first) & (key_at <= query_at), 0.0, MASKED)
 
         def some_heads(i, carry):
-            for n in range(HEADS_AT_ONCE):
-                h = i * HEADS_AT_ONCE + n
-                lanes = pl.ds(pl.multiple_of(h * HEAD_WIDTH, HEAD_WIDTH), HEAD_WIDTH)
-                attended[:rows, lanes] = attend(
-                    rotate(q[pl.ds(base, rows), lanes], cs[pl.ds(base, rows), :]),
-                    k_rot[pl.ds(low, window), :],
-                    v_ext[pl.ds(low, window), :],
-                    bias[:rows, :window],
-                )
+            lanes = [
+                pl.ds(pl.multiple_of((i * HEADS_AT_ONCE + n) * HEAD_WIDTH, HEAD_WIDTH), HEAD_WIDTH)
+                for n in range(HEADS_AT_ONCE)
+            ]
+            turn = cs[pl.ds(base, rows), :]
+            found = attend(
+                [rotate(q[pl.ds(base, rows), lane], turn) for lane in lanes],
+                k_rot[pl.ds(low, window), :],
+                v_ext[pl.ds(low, window), :],
+                bias[:rows, :window],
+            )
+            for lane, got in zip(lanes, found):
+                attended[at : at + rows, lane] = got
             return carry
 
         turns = heads // HEADS_AT_ONCE
@@ -232,19 +244,19 @@
         else:
             lax.fori_loop(0, turns, some_heads, 0)
 
-    def project(s, p):
-        return dot(attended[: parts[s][1], :], ow[:, p * step : (p + 1) * step])
+    def project(rows, p):
+        return dot(attended[:rows, :], ow[:, p * step : (p + 1) * step])
 
     def send_far(s):
         rows = parts[s][1]
         for p in range(PIECES):
-            b1_send[s, p, :rows] = project(s, p).astype(BF16)
+            b1_send[s, p, :rows] = project(rows, p).astype(BF16)
             copy_b1[s][p].start()
 
     def send_peer(s):
         rows = parts[s][1]
         for p in range(PIECES):
-            share = project(s, p)
+            share = project(rows, p)
             copy_b1[s][p].wait_recv()
             b2_send[s, p, :rows] = (share + b1_recv[s, p, :rows].astype(F32)).astype(BF16)
             copy_b2[s][p].start()
@@ -291,24 +303,22 @@
     attend_part(peer, 1, (experts, forward_c))
     send_peer(1)
 
-    for s in range(len(parts)):
-        attend_part(sib, s)
-        for p in range(PIECES):
-            b3_send[s, p, : parts[s][1]] = project(s, p).astype(BF16)
-            copy_b3[s][p].start()
-    for s, (offset, rows, _) in enumerate(parts):
-        attend_part(me, s)
-        for p in range(PIECES):
-            columns = slice(p * step, (p + 1) * step)
-            own_f[s, p, :rows] = project(s, p) + res[offset : offset + rows, columns].astype(F32)
+    for s, (offset, _, _) in enumerate(parts):
+        attend_part(sib, s, at=offset)
+    for p in range(PIECES):
+        b3_send[p] = project(chunk, p).astype(BF16)
+        copy_b3[p].start()
+    for s, (offset, _, _) in enumerate(parts):
+        attend_part(me, s, at=offset)
+    for p in range(PIECES):
+        own_f[p] = project(chunk, p) + res[:, p * step : (p + 1) * step].astype(F32)
 
     copy_c2.wait_recv()
     ysum[core] = (c2_send[...].astype(F32) + c2_recv[...].astype(F32)).astype(BF16)
     copy_c3.start()
-    for s, (_, rows, _) in enumerate(parts):
-        for p in range(PIECES):
-            copy_b3[s][p].wait_recv()
-            own_f[s, p, :rows] = own_f[s, p, :rows] + b3_recv[s, p, :rows].astype(F32)
+    for p in range(PIECES):
+        copy_b3[p].wait_recv()
+        own_f[p] = own_f[p] + b3_recv[p].astype(F32)
     copy_c3.wait_recv()
     for s, (offset, rows, _) in enumerate(parts):
         mine = pl.ds(pl.multiple_of(me * chunk + offset, 16), rows)
@@ -324,28 +334,34 @@
                 for e in range(2)
             )
             copy_b2[s][p].wait_recv()
-            mixed = own_f[s, p, :rows] + b2_recv[s, p, :rows].astype(F32)
+            mixed = own_f[p, offset : offset + rows] + b2_recv[s, p, :rows].astype(F32)
             mixed = mixed.astype(BF16).astype(F32)
             out_ref[offset : offset + rows, p * step : (p + 1) * step] = (mixed + given).astype(BF16)
 
-    for copy in [copy_a1, copy_a2, copy_a3, copy_c1, copy_c2, copy_c3]:
+    for copy in [copy_a1, copy_a2, copy_a3, copy_c1, copy_c2, copy_c3] + copy_b3:
         copy.wait_send()
-    for copies in copy_b1 + copy_b2 + copy_b3:
+    for copies in copy_b1 + copy_b2:
         for copy in copies:
             copy.wait_send()
 
 
-def hand_over(src, dst, sem):
+def hand_over(src, dst, held, sem):
     rows = src.shape[0] // COPIES
-    copies = [
-        pltpu.make_async_copy(
-            src.at[pl.ds(i * rows, rows)], dst.at[pl.ds(i * rows, rows)], sem.at[i]
-        )
-        for i in range(COPIES)
+    spans = [pl.ds(i * rows, rows) for i in range(COPIES)]
+    into = [
+        pltpu.make_async_copy(src.at[span], held.at[span], sem.at[0, i])
+        for i, span in enumerate(spans)
     ]
-    for copy in copies:
+    out = [
+        pltpu.make_async_copy(held.at[span], dst.at[span], sem.at[1, i])
+        for i, span in enumerate(spans)
+    ]
+    for copy in into:
         copy.start()
-    for copy in copies:
+    for first, second in zip(into, out):
+        first.wait()
+        second.start()
+    for copy in out:
         copy.wait()
 
 
@@ -383,6 +399,7 @@
     half = model // 2
     dma = pltpu.SemaphoreType.DMA
     pieces = (2, PIECES, most, step)
+    whole = (PIECES, chunk, step)
     gate_up = jnp.swapaxes(gate_up, 2, 3)
     scratch = [
         pltpu.VMEM((tokens, width), BF16),
@@ -398,7 +415,7 @@
         pltpu.VMEM((tokens, 2 * HEAD_WIDTH), F32),
         pltpu.VMEM((slots, tokens), F32),
         pltpu.VMEM((most, window), F32),
-        pltpu.VMEM((max(most, slots), width), BF16),
+        pltpu.VMEM((max(chunk, slots), width), BF16),
         pltpu.VMEM((slots, half), F32),
         pltpu.VMEM((slots, half), BF16),
         pltpu.VMEM((slots, half), BF16),
@@ -412,9 +429,9 @@
         pltpu.VMEM(pieces, BF16),
         pltpu.VMEM(pieces, BF16),
         pltpu.VMEM(pieces, BF16),
-        pltpu.VMEM(pieces, BF16),
-        pltpu.VMEM(pieces, BF16),
-        pltpu.VMEM(pieces, F32),
+        pltpu.VMEM(whole, BF16),
+        pltpu.VMEM(whole, BF16),
+        pltpu.VMEM(whole, F32),
         dma((3, 2, PIECES)),
         dma((3, 2, PIECES)),
         pltpu.VMEM((2, slots, half), F32),
@@ -448,7 +465,7 @@
         out_shape=jax.ShapeDtypeStruct((chunk, model), BF16),
         in_specs=[hbm],
         out_specs=hbm,
-        scratch_shapes=[dma((COPIES,))],
+        scratch_shapes=[pltpu.VMEM((chunk, model), BF16), dma((2, COPIES))],
     )(result)
 
 

time: 81 us -> 51.7 us (0.64)
  Pallas kernels: 80.7 us -> 51.4 us
    pallas_call x1, Pallas kernels: 30.9 us -> 2.05 us  [local(): pl.pallas_call(hand_over, out_shape=jax.ShapeDtypeStruct((chunk, model),...]
where the time goes in v3:
time: 51.7 us; the launch traced here: 51.6 us
  Pallas kernels  51.4 us (99%)
    pallas_call x1, Pallas kernels, local(): pl.pallas_call(functools.partial(layer_kernel, slots, parts), out_shape=j...  49.3 us
    pallas_call x1, Pallas kernels, local(): pl.pallas_call(hand_over, out_shape=jax.ShapeDtypeStruct((chunk, model),...  2.05 us

profile of v3, /device:TPU:0, one launch (start us, length us, event | category | flops | bytes accessed | tf_op | source)
XLA Modules:
  0.0 51.6 jit_solution(16531134546227210176)
XLA Ops:
  0.0 49.3 %shard_map.118.src = bf16[240,2048]{1,0:T(8,128)(2,1)} custom-call(s32[1,960]{1,0:T(1,128)} %bitcast.9, s32[8,960]{1,0:T(8,128)} %bitcast.6, f32[8,960]{1,0:T(8,128)} %bitcast.7, f32[480,256]{1,0:T(8,128)} %constant.2.clone.table_ref, f32[1,2048]{1,0:T(1,128)} %bitcast.8, bf16[960,128]{1,0:T(8,128)(2,1)} %k_ref.1, bf16[960,128]{1,0:T(8,128)(2,1)} %v_ref.1, ...), custom_call_target="tpu_custom_call" | custom-call | flops 14000000000 | bytes 14000000 | tf_op jit(solution)/shard_map/pallas_call | solution.py:446
  49.3 2.0 %shard_map.119 = bf16[240,2048]{1,0:T(8,128)(2,1)} custom-call(bf16[240,2048]{1,0:T(8,128)(2,1)} %shard_map.118.src), custom_call_target="tpu_custom_call" | custom-call | tf_op jit(solution)/shard_map/pallas_call | solution.py:463

commit v4 on v3

--- a/solution.py
+++ b/solution.py
@@ -44,6 +44,7 @@
     seg_ref, ids_ref, gw_ref, table_ref, gain_ref, k_ref, v_ref,
     q_hbm, res_hbm, ow_hbm, gu_hbm, dw_hbm,
     out_ref,
+    out, given, out_sem,
     q, res, ow, gu, dw, load_sem,
     rows_ref, cols_ref, k_rot, v_ext, cs, bias_sel, bias, attended,
     sel_f, a1_send, a1_recv, a2_send, a2_recv, mixsel, xs, a_ssem, a_rsem,
@@ -59,6 +60,7 @@
     tokens, width = q.shape
     heads = width // HEAD_WIDTH
     chunk, model = out_ref.shape
+    most = parts[0][1]
     step = model // PIECES
     half = model // 2
     cap = slots // 2
@@ -69,8 +71,7 @@
             [(q_hbm, q), (ow_hbm, ow), (res_hbm, res), (gu_hbm, gu), (dw_hbm, dw)]
         )
     ]
-    for load in loads:
-        load.start()
+    loads[0].start()
 
     barrier = pltpu.get_barrier_semaphore()
     for other in (sib, peer):
@@ -108,6 +109,9 @@
     copy_c1 = remote(c1_send, c1_recv, c_ssem.at[0], c_rsem.at[0], sib)
     copy_c2 = remote(c2_send, c2_recv, c_ssem.at[1], c_rsem.at[1], peer)
     copy_c3 = remote(ysum.at[core], ysum.at[core], c_ssem.at[2], c_rsem.at[2], sib)
+
+    loads[1].start()
+    loads[2].start()
 
     seg = seg_ref[...]
     prompts = lax.broadcasted_iota(jnp.int32, (8, tokens), 0)
@@ -193,6 +197,8 @@
             attended[:slots, lane] = got
     loads[1].wait()
     loads[2].wait()
+    loads[3].start()
+    loads[4].start()
     own_tokens = (lax.broadcasted_iota(jnp.int32, (slots, chunk), 1) + me * chunk).astype(F32)
     own_pick = (own_tokens == jnp.concatenate(idents, axis=0)).astype(F32).astype(BF16)
 
@@ -244,8 +250,8 @@
         else:
             lax.fori_loop(0, turns, some_heads, 0)
 
-    def project(rows, p):
-        return dot(attended[:rows, :], ow[:, p * step : (p + 1) * step])
+    def project(rows, p, at=0):
+        return dot(attended[at : at + rows, :], ow[:, p * step : (p + 1) * step])
 
     def send_far(s):
         rows = parts[s][1]
@@ -253,13 +259,14 @@
             b1_send[s, p, :rows] = project(rows, p).astype(BF16)
             copy_b1[s][p].start()
 
-    def send_peer(s):
+    def send_peer(s, at_once):
         rows = parts[s][1]
         for p in range(PIECES):
             share = project(rows, p)
             copy_b1[s][p].wait_recv()
             b2_send[s, p, :rows] = (share + b1_recv[s, p, :rows].astype(F32)).astype(BF16)
-            copy_b2[s][p].start()
+            if p < at_once:
+                copy_b2[s][p].start()
 
     def nothing():
         pass
@@ -294,19 +301,21 @@
     attend_part(far, 0, (forward_a, nothing))
     send_far(0)
     attend_part(peer, 0)
-    send_peer(0)
+    send_peer(0, PIECES)
     attend_part(far, 1)
     send_far(1)
     copy_a2.wait_recv()
     mixsel[core] = (a2_send[...].astype(F32) + a2_recv[...].astype(F32)).astype(BF16)
     copy_a3.start()
-    attend_part(peer, 1, (experts, forward_c))
-    send_peer(1)
-
-    for s, (offset, _, _) in enumerate(parts):
-        attend_part(sib, s, at=offset)
+    attend_part(sib, 0, (experts, forward_c), at=most)
+    attend_part(peer, 1)
+    send_peer(1, 1)
+    attend_part(sib, 1, at=most + parts[1][0])
+    copy_c2.wait_send()
+    for copy in copy_b2[1][1:]:
+        copy.start()
     for p in range(PIECES):
-        b3_send[p] = project(chunk, p).astype(BF16)
+        b3_send[p] = project(chunk, p, most).astype(BF16)
         copy_b3[p].start()
     for s, (offset, _, _) in enumerate(parts):
         attend_part(me, s, at=offset)
@@ -319,30 +328,39 @@
     for p in range(PIECES):
         copy_b3[p].wait_recv()
         own_f[p] = own_f[p] + b3_recv[p].astype(F32)
+    mine = pl.ds(pl.multiple_of(me * chunk, 16), chunk)
+    slot_lane = lax.broadcasted_iota(jnp.int32, (chunk, cap), 1).astype(F32)
+    spread = jnp.concatenate(
+        [(cols_ref[mine, e : e + 1] == slot_lane).astype(F32).astype(BF16) for e in range(2)], axis=1
+    )
     copy_c3.wait_recv()
+    for p in range(PIECES):
+        inner = p % (PIECES // 2) * step
+        given[p] = dot(spread, ysum[p * 2 // PIECES, :, inner : inner + step])
+    written = []
     for s, (offset, rows, _) in enumerate(parts):
-        mine = pl.ds(pl.multiple_of(me * chunk + offset, 16), rows)
-        slot_lane = lax.broadcasted_iota(jnp.int32, (rows, cap), 1).astype(F32)
-        spread = [
-            (cols_ref[mine, e : e + 1] == slot_lane).astype(F32).astype(BF16) for e in range(2)
-        ]
+        span = slice(offset, offset + rows)
         for p in range(PIECES):
-            inner = p % (PIECES // 2) * step
-            side = p * 2 // PIECES
-            given = sum(
-                dot(spread[e], ysum[side, e * cap : (e + 1) * cap, inner : inner + step])
-                for e in range(2)
+            copy_b2[s][p].wait_recv()
+            mixed = own_f[p, span] + b2_recv[s, p, :rows].astype(F32)
+            mixed = mixed.astype(BF16).astype(F32)
+            columns = pl.ds(p * step, step)
+            out[span, p * step : (p + 1) * step] = (mixed + given[p, span]).astype(BF16)
+            done = pltpu.make_async_copy(
+                out.at[pl.ds(offset, rows), columns],
+                out_ref.at[pl.ds(offset, rows), columns],
+                out_sem.at[s, p],
             )
-            copy_b2[s][p].wait_recv()
-            mixed = own_f[p, offset : offset + rows] + b2_recv[s, p, :rows].astype(F32)
-            mixed = mixed.astype(BF16).astype(F32)
-            out_ref[offset : offset + rows, p * step : (p + 1) * step] = (mixed + given).astype(BF16)
-
-    for copy in [copy_a1, copy_a2, copy_a3, copy_c1, copy_c2, copy_c3] + copy_b3:
+            done.start()
+            written.append(done)
+
+    for copy in [copy_a1, copy_a2, copy_a3, copy_c1, copy_c3] + copy_b3:
         copy.wait_send()
     for copies in copy_b1 + copy_b2:
         for copy in copies:
             copy.wait_send()
+    for done in written:
+        done.wait()
 
 
 def hand_over(src, dst, held, sem):
@@ -402,6 +420,9 @@
     whole = (PIECES, chunk, step)
     gate_up = jnp.swapaxes(gate_up, 2, 3)
     scratch = [
+        pltpu.VMEM((chunk, model), BF16),
+        pltpu.VMEM(whole, F32),
+        dma((2, PIECES)),
         pltpu.VMEM((tokens, width), BF16),
         pltpu.VMEM(residual_in.shape, BF16),
         pltpu.VMEM(out_weight.shape, BF16),
@@ -415,7 +436,7 @@
         pltpu.VMEM((tokens, 2 * HEAD_WIDTH), F32),
         pltpu.VMEM((slots, tokens), F32),
         pltpu.VMEM((most, window), F32),
-        pltpu.VMEM((max(chunk, slots), width), BF16),
+        pltpu.VMEM((max(most + chunk, slots), width), BF16),
         pltpu.VMEM((slots, half), F32),
         pltpu.VMEM((slots, half), BF16),
         pltpu.VMEM((slots, half), BF16),
@@ -447,7 +468,7 @@
         functools.partial(layer_kernel, slots, parts),
         out_shape=jax.ShapeDtypeStruct((chunk, model), BF16),
         in_specs=[vmem] * 7 + [hbm] * 5,
-        out_specs=vmem,
+        out_specs=hbm,
         scratch_shapes=scratch,
         compiler_params=pltpu.CompilerParams(
             collective_id=0, has_side_effects=True, vmem_limit_bytes=56 * 1024 * 1024

time: 51.7 us -> 51.4 us (level)
  no operation moved by 1% of the time
where the time goes in v4:
time: 51.4 us; the launch traced here: 51.3 us
  Pallas kernels  51.1 us (99%)
    pallas_call x1, Pallas kernels, local(): pl.pallas_call(functools.partial(layer_kernel, slots, parts), out_shape=j...  49.1 us
    pallas_call x1, Pallas kernels, local(): pl.pallas_call(hand_over, out_shape=jax.ShapeDtypeStruct((chunk, model),...  2.05 us

profile of v4, /device:TPU:0, one launch (start us, length us, event | category | flops | bytes accessed | tf_op | source)
XLA Modules:
  0.0 51.3 jit_solution(8213276101415529889)
XLA Ops:
  0.0 49.1 %shard_map.118.src = bf16[240,2048]{1,0:T(8,128)(2,1)} custom-call(s32[1,960]{1,0:T(1,128)} %bitcast.9, s32[8,960]{1,0:T(8,128)} %bitcast.6, f32[8,960]{1,0:T(8,128)} %bitcast.7, f32[480,256]{1,0:T(8,128)} %constant.2.clone.table_ref, f32[1,2048]{1,0:T(1,128)} %bitcast.8, bf16[960,128]{1,0:T(8,128)(2,1)} %k_ref.1, bf16[960,128]{1,0:T(8,128)(2,1)} %v_ref.1, ...), custom_call_target="tpu_custom_call" | custom-call | flops 14000000000 | bytes 14000000 | tf_op jit(solution)/shard_map/pallas_call | solution.py:467
  49.1 2.0 %shard_map.119 = bf16[240,2048]{1,0:T(8,128)(2,1)} custom-call(bf16[240,2048]{1,0:T(8,128)(2,1)} %shard_map.118.src), custom_call_target="tpu_custom_call" | custom-call | tf_op jit(solution)/shard_map/pallas_call | solution.py:484
